TPU v7x, 32 devices: a whole 2x2x4 slice. The times are simulated.
32 devices in a mesh: ma: 8 (over z, x), ao: 4 (over y, core).
Axes of the slice: x: 2, y: 2, z: 4, core: 2. Of those that a mesh axis runs over, the one named last changes fastest.
Arguments:
- truth_table: bfloat16 [4, 512, 512, 128], P('ao', 'ma'), may hold values from -1 to 1, as said below
- pair_list: int32 [4], replicated, may hold values from 0 to 3, as said below
Outputs:
- cross_corr: float32 [4, 512, 512, 128], P('ao', 'ma')
Inputs may be any that keep to these rules, and one draw needn't show every extreme that they name: `truth_table`: every entry is +1 or -1. `pair_list`: each output's partner is another output, and every output is the partner of exactly one output.
All inputs are finite; a program needn't handle non-finite values.
Results may differ from a plain program's by a relative error of at most 0.0003.
Values sent between devices are 32-bit elements; how exact they have to be, the bound alone decides.
A program may use at most 192 MiB of HBM per device.

v0:
```python
import jax
import jax.numpy as jnp
from jax import lax
from jax.sharding import PartitionSpec as P


def sylvester(length):
    index_row = jnp.arange(length, dtype=jnp.int32)
    shared = jnp.bitwise_and(index_row[:, None], index_row[None, :])
    ones_count = jnp.zeros((length, length), jnp.int32)
    for position in range(length.bit_length() - 1):
        ones_count = ones_count + jnp.bitwise_and(jnp.right_shift(shared, position), 1)
    return (1 - 2 * (ones_count % 2)).astype(jnp.float32)


def apply_low(field, h_low):
    return jnp.einsum("abj,jc->abc", field, h_low, precision=lax.Precision.HIGHEST)


def apply_mid(field, h_mid):
    return jnp.einsum("bj,ajc->abc", h_mid, field, precision=lax.Precision.HIGHEST)


def apply_high(field, h_high, factor):
    return jnp.einsum("ai,ibc->abc", h_high, field, precision=lax.Precision.HIGHEST) * factor


def signs_low(table, h_low_half):
    return jnp.einsum("abj,jc->abc", table, h_low_half, preferred_element_type=jnp.float32)


def signs_mid(field, h_mid_half):
    return jnp.einsum("bj,ajc->abc", h_mid_half, field, preferred_element_type=jnp.float32)


def partner_gathered(spectrum, pair_list):
    mine = lax.axis_index("ao")
    mate = pair_list[mine]
    piece = lax.all_gather(spectrum[None], "ao", axis=0, tiled=True)
    start = jnp.int32(0)
    count = piece.shape[0]
    offset = jnp.clip(mate, 0, count - 1)
    chosen = lax.dynamic_index_in_dim(piece, offset, 0, keepdims=False)
    found = jnp.logical_and(mate >= start, mate < start + count)
    mates = jnp.where(found, chosen, jnp.zeros_like(spectrum))
    return spectrum * mates


def pair_product(spectrum, pair_list):
    return partner_gathered(spectrum, pair_list)


def body(truth_table, pair_list):
    table = truth_table[0]
    rows_here = table.shape[0]
    mid_len = table.shape[1]
    low_len = table.shape[2]
    high_len = rows_here * lax.axis_size("ma")
    factor = 1.0 / jnp.sqrt(jnp.float32(high_len * mid_len * low_len))
    h_high = sylvester(high_len)
    h_mid = sylvester(mid_len)
    h_low = sylvester(low_len)

    def high_step(field):
        return apply_high(field, h_high, factor)

    first_pass = signs_low(table, h_low.astype(jnp.bfloat16)).astype(jnp.bfloat16)
    partial_spec = signs_mid(first_pass, h_mid.astype(jnp.bfloat16))
    spectrum = high_step(
        lax.all_to_all(partial_spec, "ma", split_axis=1, concat_axis=0, tiled=True)
    )
    spectrum = lax.all_to_all(spectrum, "ma", split_axis=0, concat_axis=1, tiled=True)
    product = pair_product(spectrum, pair_list)
    product = apply_mid(apply_low(product, h_low), h_mid)
    mixed = high_step(lax.all_to_all(product, "ma", split_axis=1, concat_axis=0, tiled=True))
    result = lax.all_to_all(mixed, "ma", split_axis=0, concat_axis=1, tiled=True)
    return result[None]


def solution(mesh):
    return jax.shard_map(
        body,
        mesh=mesh,
        in_specs=(P("ao", "ma", None, None), P()),
        out_specs=P("ao", "ma", None, None),
        check_vma=False,
    )
```

profile of v0, /device:TPU:0, one launch (start us, length us, event | category | flops | bytes accessed | tf_op | source)
XLA Modules:
  0.0 2102.0 jit_solution(368012756062145836)
XLA Ops:
  6.5 0.0 all-gather.2.cloned.1.call-start
  6.5 13.9 convolution_bitcast_fusion.1
  20.5 16.6 copy.24
  37.0 370.1 %all_to_all.69 = f32[64,512,128]{2,0,1:T(8,128)S(1)} all-to-all(f32[64,512,128]{2,0,1:T(8,128)} %copy.24), channel_id=1, replica_groups=mesh['ma'=8,'ao'=4] {'ma'}, dimensions={1} | all-to-all | bytes 33554432 | tf_op jit(solution)/shard_map/all_to_all | solution.py:70
  407.1 1.7 copy.26
  408.8 32.4 %convolution_multiply_fusion.1 = f32[512,64,128]{2,0,1:T(8,128)S(1)} fusion(f32[512,64,128]{2,0,1:T(8,128)S(1)} %bitcast.58), kind=kOutput, calls=%fused_computation.5 | convolution fusion | flops 25784745984 | bytes 33554432 | tf_op jit(solution)/shard_map/ai,ibc->abc/dot_general | solution.py:25
  441.2 18.1 copy.27
  459.3 366.6 %all_to_all.70 = f32[512,64,128]{2,1,0:T(8,128)S(1)} all-to-all(f32[512,64,128]{2,1,0:T(8,128)S(1)} %copy.27), channel_id=1, replica_groups=mesh['ma'=8,'ao'=4] {'ma'}, dimensions={0} | all-to-all | bytes 33554432 | tf_op jit(solution)/shard_map/all_to_all | solution.py:72
  825.9 6.2 copy.28
  832.1 0.0 copy-start
  832.1 0.0 all-gather.2.cloned.1.call-update
  832.2 0.6 copy-done
  832.8 0.6 dynamic_slice.7
  835.3 388.0 %all-gather.2.cloned.1.call-done = f32[4,64,512,128]{3,2,1,0:T(8,128)} async-done(((f32[1,64,512,128]{3,2,1,0:T(8,128)}), f32[4,64,512,128]{3,2,1,0:T(8,128)}) %all-gather.2.cloned.1.call-update) | async-done | bytes 67108880 | tf_op jit(solution)/shard_map/all_gather | solution.py:39
  1223.3 24.5 %fusion = f32[64,512,128]{1,2,0:T(8,128)} fusion(f32[64,512,128]{2,1,0:T(8,128)} %bitcast.57, f32[4,64,512,128]{3,2,1,0:T(8,128)} %all-gather.2.cloned.1.call-done, s32[]{:T(128)} %bitcast.16, pred[]{:T(512)} %bitcast.13), kind=kOutput, calls=%fused_computation.1 | convolution fusion | flops 6451412992 | bytes 50332672 | tf_op jit(solution)/shard_map/abj,jc->abc/dot_general | solution.py:17
  1247.8 37.6 %convolution_bitcast_fusion = f32[64,512,128]{1,2,0:T(8,128)} fusion(f32[64,512,128]{1,2,0:T(8,128)} %fusion), kind=kOutput, calls=%fused_computation.6 | convolution fusion | flops 25780551680 | bytes 33554432 | tf_op jit(solution)/shard_map/bj,ajc->abc/dot_general | solution.py:21
  1285.4 16.6 copy.31
  1302.0 368.7 %all_to_all.71 = f32[64,512,128]{2,0,1:T(8,128)S(1)} all-to-all(f32[64,512,128]{2,0,1:T(8,128)} %copy.31), channel_id=1, replica_groups=mesh['ma'=8,'ao'=4] {'ma'}, dimensions={1} | all-to-all | bytes 33554432 | tf_op jit(solution)/shard_map/all_to_all | solution.py:75
  1670.7 1.7 copy.33
  1672.4 31.9 %convolution_multiply_fusion = f32[512,64,128]{2,0,1:T(8,128)S(1)} fusion(f32[512,64,128]{2,0,1:T(8,128)S(1)} %bitcast.59), kind=kOutput, calls=%fused_computation.4 | convolution fusion | flops 25784745984 | bytes 33554432 | tf_op jit(solution)/shard_map/ai,ibc->abc/dot_general | solution.py:25
  1704.3 18.1 copy.34
  1722.4 366.3 %all_to_all.72 = f32[512,64,128]{2,1,0:T(8,128)S(1)} all-to-all(f32[512,64,128]{2,1,0:T(8,128)S(1)} %copy.34), channel_id=1, replica_groups=mesh['ma'=8,'ao'=4] {'ma'}, dimensions={0} | all-to-all | bytes 33554432 | tf_op jit(solution)/shard_map/all_to_all | solution.py:76
  2088.7 6.2 copy.35
Async XLA Ops:
  6.5 1216.8 %all-gather.2.cloned.1.call-start = ((), (), s32[]{:S(2)}) async-start(), calls=%async_computation.4 | async-start | bytes 83886080 | tf_op jit(solution)/shard_map/all_gather | solution.py:39
  832.1 0.7 copy-start
Sparse Core Ops, SparseCore 0:
  832.3 390.9 all-gather.1
where the time goes:
time: 2110 us; the launch traced here: 2100 us
  blocking collectives  1470 us (70%)
  waiting for transfers between devices  388 us (18%)
  matrix products  140 us (7%)
  local copies, waits for them, and re-layouts  86.4 us (4%)
    all_gather x1, waiting for transfers between devices, partner_gathered(): piece = lax.all_gather(spectrum[None], 'ao', axis=0, tiled=True)  388 us
    all_to_all x1, blocking collectives, body(): lax.all_to_all(partial_spec, 'ma', split_axis=1, concat_axis=0, tiled=True)  370 us
    all_to_all x1, blocking collectives, body(): lax.all_to_all(product, 'ma', split_axis=1, concat_axis=0, tiled=True)  369 us
    all_to_all x1, blocking collectives, body(): lax.all_to_all(spectrum, 'ma', split_axis=0, concat_axis=1, tiled=True)  367 us
    all_to_all x1, blocking collectives, body(): lax.all_to_all(mixed, 'ma', split_axis=0, concat_axis=1, tiled=True)  366 us
    dot_general x2, matrix products, apply_high(): jnp.einsum('ai,ibc->abc', h_high, field, precision=lax.Precision.HIGHEST)  64.3 us
  transfers between devices with their start and end apart: 1, of which 1 were waited for; matrix products, arithmetic and copies ran while one was open for 0% of the time, Pallas kernels for 0%

commit v1 on v0

--- a/solution.py
+++ b/solution.py
@@ -36,7 +36,46 @@
 def partner_gathered(spectrum, pair_list):
     mine = lax.axis_index("ao")
     mate = pair_list[mine]
-    piece = lax.all_gather(spectrum[None], "ao", axis=0, tiled=True)
+
+    def _post_packet(axis_no, piece_in):
+        x_now, current_value, now = (
+            lax.axis_size("ao"),
+            lax.axis_index("ao"),
+            piece_in.shape[axis_no],
+        )
+        wide_out = lax.dynamic_update_slice_in_dim(
+            jnp.zeros(
+                tuple(
+                    (j * x_now if to_i == axis_no else j for to_i, j in enumerate(piece_in.shape))
+                ),
+                piece_in.dtype,
+            ),
+            piece_in,
+            current_value * now,
+            axis=axis_no,
+        )
+        current_arr = g_now = piece_in
+        for dev_i in [*range(1, x_now // 2 + 1)]:
+            current_arr = lax.ppermute(
+                current_arr,
+                axis_name="ao",
+                perm=tuple(((to_i, (to_i + 1) % x_now) for to_i in range(x_now))),
+            )
+            wide_out = lax.dynamic_update_slice_in_dim(
+                wide_out, current_arr, (current_value - dev_i) % x_now * now, axis=axis_no
+            )
+            if 2 * dev_i < x_now:
+                g_now = lax.ppermute(
+                    g_now,
+                    axis_name="ao",
+                    perm=tuple(((to_i, (to_i - 1) % x_now) for to_i in range(x_now))),
+                )
+                wide_out = lax.dynamic_update_slice_in_dim(
+                    wide_out, g_now, (current_value + dev_i) % x_now * now, axis=axis_no
+                )
+        return wide_out
+
+    piece = _post_packet(0, spectrum[None])
     start = jnp.int32(0)
     count = piece.shape[0]
     offset = jnp.clip(mate, 0, count - 1)

time: 2110 us -> 2270 us (1.076)
  waiting for transfers between devices: 388 us -> 484 us
  local copies, waits for them, and re-layouts: 86.4 us -> 153 us
    ppermute x0 -> x3, waiting for transfers between devices: none -> 484 us  [the longest x2 484 us: _post_packet(): lax.ppermute(current_arr, axis_name='ao', perm=tuple(((to_i, (to_i + 1) %...]
    all_gather x1 -> x0, waiting for transfers between devices: 388 us -> none  [partner_gathered(): piece = lax.all_gather(spectrum[None], 'ao', axis=0, tiled=True)]
    dynamic_update_slice x0 -> x4, local copies, waits for them, and re-layouts: none -> 45.8 us  [the longest x2 22.9 us: _post_packet(): lax.dynamic_update_slice_in_dim(wide_out, current_arr, (current_value - d...]
  transfers between devices with their start and end apart: 1 -> 3, of which waited for: 1 -> 2; matrix products, arithmetic and copies ran while one was open for 0% -> 2% of each run, Pallas kernels for 0% -> 0%
where the time goes in v1:
time: 2270 us; the launch traced here: 2260 us
  blocking collectives  1470 us (65%)
  waiting for transfers between devices  484 us (21%)
  local copies, waits for them, and re-layouts  153 us (7%)
  matrix products  152 us (7%)
    ppermute x2, waiting for transfers between devices, _post_packet(): lax.ppermute(current_arr, axis_name='ao', perm=tuple(((to_i, (to_i + 1) %...  484 us
    all_to_all x1, blocking collectives, body(): lax.all_to_all(partial_spec, 'ma', split_axis=1, concat_axis=0, tiled=True)  370 us
    all_to_all x1, blocking collectives, body(): lax.all_to_all(product, 'ma', split_axis=1, concat_axis=0, tiled=True)  367 us
    all_to_all x1, blocking collectives, body(): lax.all_to_all(spectrum, 'ma', split_axis=0, concat_axis=1, tiled=True)  367 us
    all_to_all x1, blocking collectives, body(): lax.all_to_all(mixed, 'ma', split_axis=0, concat_axis=1, tiled=True)  366 us
    dot_general x2, matrix products, apply_high(): jnp.einsum('ai,ibc->abc', h_high, field, precision=lax.Precision.HIGHEST)  76.1 us
  transfers between devices with their start and end apart: 3, of which 2 were waited for; matrix products, arithmetic and copies ran while one was open for 2% of the time, Pallas kernels for 0%

profile of v1, /device:TPU:0, one launch (start us, length us, event | category | flops | bytes accessed | tf_op | source)
XLA Modules:
  0.0 2263.6 jit_solution(17954408230203398667)
XLA Ops:
  0.0 13.9 convolution_bitcast_fusion.1
  13.9 16.6 copy.24
  30.4 370.1 %all_to_all.69 = f32[64,512,128]{2,0,1:T(8,128)S(1)} all-to-all(f32[64,512,128]{2,0,1:T(8,128)} %copy.24), channel_id=1, replica_groups=mesh['ma'=8,'ao'=4] {'ma'}, dimensions={1} | all-to-all | bytes 33554432 | tf_op jit(solution)/shard_map/all_to_all | solution.py:109
  400.6 1.7 copy.26
  402.3 44.1 %convolution_multiply_fusion.1 = f32[512,64,128]{2,0,1:T(8,128)S(1)} fusion(f32[512,64,128]{2,0,1:T(8,128)S(1)} %bitcast.56), kind=kOutput, calls=%fused_computation.5 | convolution fusion | flops 25784745984 | bytes 33554432 | tf_op jit(solution)/shard_map/ai,ibc->abc/dot_general | solution.py:25
  446.5 18.1 copy.27
  464.6 366.6 %all_to_all.70 = f32[512,64,128]{2,1,0:T(8,128)S(1)} all-to-all(f32[512,64,128]{2,1,0:T(8,128)S(1)} %copy.27), channel_id=1, replica_groups=mesh['ma'=8,'ao'=4] {'ma'}, dimensions={0} | all-to-all | bytes 33554432 | tf_op jit(solution)/shard_map/all_to_all | solution.py:111
  831.2 0.0 copy-start
  831.2 6.2 copy.28
  837.4 0.0 collective-permute-start
  837.4 1.7 collective-permute-start.1
  839.2 359.3 %collective-permute-done = f32[1,64,512,128]{3,2,1,0:T(8,128)} collective-permute-done((f32[1,64,512,128]{3,2,1,0:T(8,128)}, f32[1,64,512,128]{3,2,1,0:T(8,128)}, u32[]{:S(2)}, u32[]{:S(2)}) %collective-permute-start) | collective-permute-done | bytes 16777248 | tf_op jit(solution)/shard_map/ppermute | solution.py:59
  1198.4 0.0 collective-permute-start.2
  1198.5 0.0 copy-done
  1198.5 0.6 dynamic_slice.7
  1200.9 21.2 broadcast_in_dim.8
  1222.1 11.5 constant_dynamic-update-slice_fusion.3
  1233.5 11.5 constant_dynamic-update-slice_fusion.2
  1245.0 0.0 collective-permute-done.1
  1245.0 11.5 constant_dynamic-update-slice_fusion.1
  1256.5 125.1 %collective-permute-done.2 = f32[1,64,512,128]{3,2,1,0:T(8,128)} collective-permute-done((f32[1,64,512,128]{3,2,1,0:T(8,128)}, f32[1,64,512,128]{3,2,1,0:T(8,128)}, u32[]{:S(2)}, u32[]{:S(2)}) %collective-permute-start.2) | collective-permute-done | bytes 16777248 | tf_op jit(solution)/shard_map/ppermute | solution.py:59
  1381.5 11.4 constant_dynamic-update-slice_fusion
  1393.0 24.5 %fusion = f32[64,512,128]{1,2,0:T(8,128)} fusion(f32[64,512,128]{2,1,0:T(8,128)} %bitcast.12, f32[4,64,512,128]{3,2,1,0:T(8,128)} %constant_dynamic-update-slice_fusion, s32[]{:T(128)} %bitcast.16, pred[]{:T(512)} %bitcast.13), kind=kOutput, calls=%fused_computation.1 | convolution fusion | flops 6451412992 | bytes 50332672 | tf_op jit(solution)/shard_map/abj,jc->abc/dot_general | solution.py:17
  1417.4 37.6 %convolution_bitcast_fusion = f32[64,512,128]{1,2,0:T(8,128)} fusion(f32[64,512,128]{1,2,0:T(8,128)} %fusion), kind=kOutput, calls=%fused_computation.6 | convolution fusion | flops 25780551680 | bytes 33554432 | tf_op jit(solution)/shard_map/bj,ajc->abc/dot_general | solution.py:21
  1455.1 16.6 copy.31
  1471.6 367.4 %all_to_all.71 = f32[64,512,128]{2,0,1:T(8,128)S(1)} all-to-all(f32[64,512,128]{2,0,1:T(8,128)} %copy.31), channel_id=1, replica_groups=mesh['ma'=8,'ao'=4] {'ma'}, dimensions={1} | all-to-all | bytes 33554432 | tf_op jit(solution)/shard_map/all_to_all | solution.py:114
  1839.0 1.7 copy.33
  1840.7 31.9 %convolution_multiply_fusion = f32[512,64,128]{2,0,1:T(8,128)S(1)} fusion(f32[512,64,128]{2,0,1:T(8,128)S(1)} %bitcast.57), kind=kOutput, calls=%fused_computation.4 | convolution fusion | flops 25784745984 | bytes 33554432 | tf_op jit(solution)/shard_map/ai,ibc->abc/dot_general | solution.py:25
  1872.7 18.1 copy.34
  1890.8 366.3 %all_to_all.72 = f32[512,64,128]{2,1,0:T(8,128)S(1)} all-to-all(f32[512,64,128]{2,1,0:T(8,128)S(1)} %copy.34), channel_id=1, replica_groups=mesh['ma'=8,'ao'=4] {'ma'}, dimensions={0} | all-to-all | bytes 33554432 | tf_op jit(solution)/shard_map/all_to_all | solution.py:115
  2257.0 6.2 copy.35
Async XLA Ops:
  831.2 367.3 %copy-start = (s32[4]{0:T(128)S(1)}, s32[4]{0:T(128)}, u32[]{:S(2)}) copy-start(s32[4]{0:T(128)} %param.3) | copy-start | bytes 52
  837.4 361.0 %collective-permute-start = (f32[1,64,512,128]{3,2,1,0:T(8,128)}, f32[1,64,512,128]{3,2,1,0:T(8,128)}, u32[]{:S(2)}, u32[]{:S(2)}) collective-permute-start(f32[1,64,512,128]{3,2,1,0:T(8,128)} %bitcast.15), channel_id=1, source_target_pairs={{0,1},{1,2},{2,3},{3,0},{4,5},{5,6},{6,7},{7,4},{8,9},{9,10},{10,1... | collective-permute-start | bytes 50331656 | tf_op jit(solution)/shard_map/ppermute | solution.py:59
  837.4 407.6 %collective-permute-start.1 = (f32[1,64,512,128]{3,2,1,0:T(8,128)}, f32[1,64,512,128]{3,2,1,0:T(8,128)}, u32[]{:S(2)}, u32[]{:S(2)}) collective-permute-start(f32[1,64,512,128]{3,2,1,0:T(8,128)} %bitcast.15), channel_id=1, source_target_pairs={{0,3},{1,0},{2,1},{3,2},{4,7},{5,4},{6,5},{7,6},{8,11},{9,8},{10,9... | collective-permute-start | bytes 50331656 | tf_op jit(solution)/shard_map/ppermute | solution.py:68
  1198.4 183.1 %collective-permute-start.2 = (f32[1,64,512,128]{3,2,1,0:T(8,128)}, f32[1,64,512,128]{3,2,1,0:T(8,128)}, u32[]{:S(2)}, u32[]{:S(2)}) collective-permute-start(f32[1,64,512,128]{3,2,1,0:T(8,128)} %collective-permute-done), channel_id=1, source_target_pairs={{0,1},{1,2},{2,3},{3,0},{4,5},{5,6},{6,7},{7,4},{8,9},{9,10},{10,1... | collective-permute-start | bytes 50331656 | tf_op jit(solution)/shard_map/ppermute | solution.py:59
